TPU v7x, 1024 devices: a whole 8x8x8 slice. The times are simulated.
1024 devices in a mesh: dp: 16 (over x, core), shard: 64 (over z, y).
Axes of the slice: x: 8, y: 8, z: 8, core: 2. Of those that a mesh axis runs over, the one named last changes fastest.
Arguments:
- momentum: float32 [4096, 7168], P('dp', 'shard'), may hold values from -6 to 6
- gradient: bfloat16 [4096, 7168], P('dp', 'shard'), may hold values from -120 to 120
Outputs:
- new_momentum: float32 [4096, 7168], P('dp', 'shard')
- update: float32 [4096, 7168], P('dp', 'shard')
All inputs are finite; a program needn't handle non-finite values.
Results may differ from a plain program's by a relative error of at most 0.0038.
The roundings to bfloat16 on the way count: a program that leaves them out, or rounds other values in their place, can miss the bound.
Values may be sent and summed in bfloat16 or wider, within the bound.
A program may use at most 32 MiB of HBM per device.

v0:
```python
import math

import jax
import jax.numpy as jnp
from jax import lax
from jax.sharding import Mesh
from jax.sharding import PartitionSpec as P

D = 7168
STEPS = 2
SHARD = ("shard_0", "shard_1")


momentum_decay = 0.95
linear_term = 3.4445
cubic_term = -4.775
quintic_term = 2.0315


def own_rows(running, axes):
    for axis in axes:
        running = lax.psum_scatter(running, axis, scatter_dimension=0, tiled=True)
    return running


def in_order(tiles, dim):
    tiles = jnp.moveaxis(tiles, 0, dim)
    dims = tiles.shape
    return tiles.reshape(*dims[:dim], dims[dim] * dims[dim + 1], *dims[dim + 2 :])


def gather_in_order(x, axes, sequence):
    tiles = x
    for k in sequence:
        tiles = lax.all_gather(tiles, axes[k])
    done = sequence[::-1]
    back = [done.index(k) for k in range(len(axes))]
    tiles = tiles.transpose(*back, *range(len(axes), tiles.ndim))
    return tiles.reshape(-1, *x.shape)


def gather_axes(x, axes, sequence, dim):
    return in_order(gather_in_order(x, axes, sequence), dim)


def from_everyone(x, axis):
    length = lax.axis_size(axis)
    return lax.all_to_all(jnp.broadcast_to(x[None], (length, *x.shape)), axis, 0, 0, tiled=True)


def of_everyone(x, axis):
    return from_everyone(x, axis).sum(axis=0)


def apply_panel(gram_panel, right_side):
    return lax.dot_general(
        gram_panel, right_side, (((0,), (0,)), ((), ())), preferred_element_type=jnp.float32
    )


def body(momentum, gradient):
    grad_full = gradient.astype(jnp.float32)
    new_momentum = momentum_decay * momentum + grad_full
    current = grad_full + momentum_decay * new_momentum
    for iteration in range(STEPS):
        matrix = current.astype(jnp.bfloat16)
        column_panel = lax.all_gather(matrix, "dp", axis=0, tiled=True)
        summed_part = own_rows(
            lax.dot_general(
                column_panel, matrix, (((1,), (1,)), ((), ())), preferred_element_type=jnp.float32
            ),
            SHARD,
        )
        gram_part = summed_part.astype(jnp.bfloat16)
        gram_panel = gather_axes(gram_part, SHARD, (0, 1), 0)
        square_sum = of_everyone(jnp.sum(jnp.square(gram_panel.astype(jnp.float32))), "dp")
        inverse_norm = lax.rsqrt(square_sum)
        root_scale = jnp.sqrt(inverse_norm)
        matrix_full = matrix.astype(jnp.float32)
        first_product = apply_panel(gram_panel, column_panel)
        mixture = (
            cubic_term * root_scale * matrix_full
            + quintic_term * root_scale * inverse_norm * first_product
        ).astype(jnp.bfloat16)
        second_product = apply_panel(gram_panel, lax.all_gather(mixture, "dp", axis=0, tiled=True))
        current = linear_term * root_scale * matrix_full + inverse_norm * second_product
    update = math.sqrt(D) * current
    return (new_momentum, update)


def solution(mesh):
    split = Mesh(mesh.devices.reshape(mesh.shape["dp"], 8, 8), ("dp", "shard_0", "shard_1"))
    return jax.shard_map(
        body,
        mesh=split,
        in_specs=(P("dp", SHARD), P("dp", SHARD)),
        out_specs=(P("dp", SHARD), P("dp", SHARD)),
        check_vma=False,
    )
```

profile of v0, /device:TPU:1, one launch (start us, length us, event | category | flops | bytes accessed | tf_op | source)
XLA Modules:
  0.0 502.8 jit_solution(13697247598753931100)
XLA Ops:
  7.2 0.0 reduce-scatter.5.cloned.1.call-start
  7.2 1.6 fusion.8
  8.8 31.3 %all_gather.36 = bf16[4096,112]{0,1:T(8,128)(2,1)S(1)} all-gather(bf16[256,112]{0,1:T(8,128)(2,1)S(1)} %get-tuple-element.2), channel_id=1, replica_groups=mesh['dp'=16,'shard_0'=8,'shard_1'=8] {'dp'}, dimensions={0}, use_global_device_ids=true | all-gather | bytes 974848 | tf_op jit(solution)/shard_map/all_gather | solution.py:67
  40.1 2.7 fusion.9
  42.8 0.0 reduce-scatter.5.cloned.1.call-update
  42.8 0.0 reduce-scatter.7.cloned.1.call-start
  42.8 60.9 %reduce-scatter.5.cloned.1.call-done = f32[512,256]{1,0:T(8,128)} async-done(((f32[4096,256]{1,0:T(8,128)}), f32[512,256]{1,0:T(8,128)}) %reduce-scatter.5.cloned.1.call-update) | async-done | bytes 524304 | tf_op jit(solution)/shard_map/reduce_scatter | solution.py:22
  103.7 0.0 reduce-scatter.7.cloned.1.call-update
  103.8 0.0 all-gather.7.cloned.1.call-start
  103.8 38.2 %reduce-scatter.7.cloned.1.call-done = f32[64,256]{1,0:T(8,128)} async-done(((f32[512,256]{1,0:T(8,128)}), f32[64,256]{1,0:T(8,128)}) %reduce-scatter.7.cloned.1.call-update) | async-done | bytes 65552 | tf_op jit(solution)/shard_map/reduce_scatter | solution.py:22
  142.0 0.8 convert_element_type.37
  142.8 24.2 %all-gather = bf16[512,256]{1,0:T(8,128)(2,1)} all-gather(bf16[64,256]{1,0:T(8,128)(2,1)S(1)} %convert_element_type.37), channel_id=2, replica_groups=mesh['dp'=16,'shard_0'=8,'shard_1'=8] {'shard_0'}, dimensions={0}, use_global_device_ids=true | all-gather | bytes 294912 | tf_op jit(solution)/shard_map/all_gather | solution.py:35
  167.1 0.0 all-gather.7.cloned.1.call-update
  167.1 50.0 %all-gather.7.cloned.1.call-done = bf16[64,64,256]{2,1,0:T(8,128)(2,1)} async-done(((bf16[8,64,256]{2,1,0:T(8,128)(2,1)}), bf16[64,64,256]{2,1,0:T(8,128)(2,1)}) %all-gather.7.cloned.1.call-update) | async-done | bytes 2097168 | tf_op jit(solution)/shard_map/all_gather | solution.py:35
  217.1 3.3 multiply_reduce_fusion.1
  220.3 1.2 broadcast_in_dim.4
  221.6 11.0 %all-to-all-start = ((f32[16,1,1]{2,1,0:T(1,128)}), f32[16,1,1]{2,1,0:T(1,128)S(1)}, u32[]{:S(2)}, u32[]{:S(2)}) async-start(f32[16,1,1]{2,1,0:T(1,128)} %broadcast_in_dim.4), calls=%async_computation.2 | async-start | bytes 16384 | tf_op jit(solution)/shard_map/all_to_all | solution.py:48
  232.6 0.0 reduce-scatter.9.cloned.1.call-start
  232.6 1.7 copy.11
  234.4 5.2 %all-to-all-done = f32[16,1,1]{2,1,0:T(1,128)S(1)} async-done(((f32[16,1,1]{2,1,0:T(1,128)}), f32[16,1,1]{2,1,0:T(1,128)S(1)}, u32[]{:S(2)}, u32[]{:S(2)}) %all-to-all-start) | async-done | bytes 96 | tf_op jit(solution)/shard_map/all_to_all | solution.py:48
  239.5 0.6 reduce_sum.37
  240.9 0.4 fusion.5
  241.3 17.7 %all_gather.41 = bf16[4096,112]{0,1:T(8,128)(2,1)S(1)} all-gather(bf16[256,112]{0,1:T(8,128)(2,1)S(1)} %fusion.5), channel_id=1, replica_groups=mesh['dp'=16,'shard_0'=8,'shard_1'=8] {'dp'}, dimensions={0}, use_global_device_ids=true | all-gather | bytes 974848 | tf_op jit(solution)/shard_map/all_gather | solution.py:85
  259.0 0.5 fusion.6
  259.5 18.1 %all_gather.42 = bf16[4096,112]{0,1:T(8,128)(2,1)S(1)} all-gather(bf16[256,112]{0,1:T(8,128)(2,1)S(1)} %fusion.6), channel_id=1, replica_groups=mesh['dp'=16,'shard_0'=8,'shard_1'=8] {'dp'}, dimensions={0}, use_global_device_ids=true | all-gather | bytes 974848 | tf_op jit(solution)/shard_map/all_gather | solution.py:67
  277.6 2.7 fusion.10
  280.3 0.0 reduce-scatter.9.cloned.1.call-update
  280.3 0.0 reduce-scatter.11.cloned.1.call-start
  280.4 58.9 %reduce-scatter.9.cloned.1.call-done = f32[512,256]{1,0:T(8,128)} async-done(((f32[4096,256]{1,0:T(8,128)}), f32[512,256]{1,0:T(8,128)}) %reduce-scatter.9.cloned.1.call-update) | async-done | bytes 524304 | tf_op jit(solution)/shard_map/reduce_scatter | solution.py:22
  339.3 0.0 reduce-scatter.11.cloned.1.call-update
  339.3 0.0 all-gather.9.cloned.1.call-start
  339.4 38.4 %reduce-scatter.11.cloned.1.call-done = f32[64,256]{1,0:T(8,128)} async-done(((f32[512,256]{1,0:T(8,128)}), f32[64,256]{1,0:T(8,128)}) %reduce-scatter.11.cloned.1.call-update) | async-done | bytes 65552 | tf_op jit(solution)/shard_map/reduce_scatter | solution.py:22
  377.8 0.8 convert_element_type.42
  378.6 24.3 %all-gather.2 = bf16[512,256]{1,0:T(8,128)(2,1)} all-gather(bf16[64,256]{1,0:T(8,128)(2,1)S(1)} %convert_element_type.42), channel_id=4, replica_groups=mesh['dp'=16,'shard_0'=8,'shard_1'=8] {'shard_0'}, dimensions={0}, use_global_device_ids=true | all-gather | bytes 294912 | tf_op jit(solution)/shard_map/all_gather | solution.py:35
  402.9 0.0 all-gather.9.cloned.1.call-update
  402.9 50.0 %all-gather.9.cloned.1.call-done = bf16[64,64,256]{2,1,0:T(8,128)(2,1)} async-done(((bf16[8,64,256]{2,1,0:T(8,128)(2,1)}), bf16[64,64,256]{2,1,0:T(8,128)(2,1)}) %all-gather.9.cloned.1.call-update) | async-done | bytes 2097168 | tf_op jit(solution)/shard_map/all_gather | solution.py:35
  452.9 3.3 multiply_reduce_fusion
  456.2 1.2 broadcast_in_dim.5
  457.4 11.0 %all-to-all-start.1 = ((f32[16,1,1]{2,1,0:T(1,128)}), f32[16,1,1]{2,1,0:T(1,128)S(1)}, u32[]{:S(2)}, u32[]{:S(2)}) async-start(f32[16,1,1]{2,1,0:T(1,128)} %broadcast_in_dim.5), calls=%async_computation.5 | async-start | bytes 16384 | tf_op jit(solution)/shard_map/all_to_all | solution.py:48
  468.4 1.8 copy.13
  470.2 5.1 %all-to-all-done.1 = f32[16,1,1]{2,1,0:T(1,128)S(1)} async-done(((f32[16,1,1]{2,1,0:T(1,128)}), f32[16,1,1]{2,1,0:T(1,128)S(1)}, u32[]{:S(2)}, u32[]{:S(2)}) %all-to-all-start.1) | async-done | bytes 96 | tf_op jit(solution)/shard_map/all_to_all | solution.py:48
  475.3 0.6 reduce_sum.39
  476.7 0.5 fusion.7
  477.1 17.7 %all_gather.47 = bf16[4096,112]{0,1:T(8,128)(2,1)S(1)} all-gather(bf16[256,112]{0,1:T(8,128)(2,1)S(1)} %fusion.7), channel_id=1, replica_groups=mesh['dp'=16,'shard_0'=8,'shard_1'=8] {'dp'}, dimensions={0}, use_global_device_ids=true | all-gather | bytes 974848 | tf_op jit(solution)/shard_map/all_gather | solution.py:85
  494.8 1.1 fusion.4
Async XLA Ops:
  7.2 96.6 %reduce-scatter.5.cloned.1.call-start = ((), (), s32[]{:S(2)}) async-start(), calls=%async_computation.6 | async-start | bytes 4718592 | tf_op jit(solution)/shard_map/reduce_scatter | solution.py:22
  42.8 99.2 %reduce-scatter.7.cloned.1.call-start = ((), (), s32[]{:S(2)}) async-start(), calls=%async_computation.7 | async-start | bytes 589824 | tf_op jit(solution)/shard_map/reduce_scatter | solution.py:22
  103.8 113.3 %all-gather.7.cloned.1.call-start = ((), (), s32[]{:S(2)}) async-start(), calls=%async_computation.10 | async-start | bytes 2359296 | tf_op jit(solution)/shard_map/all_gather | solution.py:35
  221.6 18.0 %all-to-all-start = ((f32[16,1,1]{2,1,0:T(1,128)}), f32[16,1,1]{2,1,0:T(1,128)S(1)}, u32[]{:S(2)}, u32[]{:S(2)}) async-start(f32[16,1,1]{2,1,0:T(1,128)} %broadcast_in_dim.4), calls=%async_computation.2 | async-start | bytes 16384 | tf_op jit(solution)/shard_map/all_to_all | solution.py:48
  232.6 106.7 %reduce-scatter.9.cloned.1.call-start = ((), (), s32[]{:S(2)}) async-start(), calls=%async_computation.8 | async-start | bytes 4718592 | tf_op jit(solution)/shard_map/reduce_scatter | solution.py:22
  280.3 97.4 %reduce-scatter.11.cloned.1.call-start = ((), (), s32[]{:S(2)}) async-start(), calls=%async_computation.9 | async-start | bytes 589824 | tf_op jit(solution)/shard_map/reduce_scatter | solution.py:22
  339.3 113.5 %all-gather.9.cloned.1.call-start = ((), (), s32[]{:S(2)}) async-start(), calls=%async_computation.11 | async-start | bytes 2359296 | tf_op jit(solution)/shard_map/all_gather | solution.py:35
  457.4 18.0 %all-to-all-start.1 = ((f32[16,1,1]{2,1,0:T(1,128)}), f32[16,1,1]{2,1,0:T(1,128)S(1)}, u32[]{:S(2)}, u32[]{:S(2)}) async-start(f32[16,1,1]{2,1,0:T(1,128)} %broadcast_in_dim.5), calls=%async_computation.5 | async-start | bytes 16384 | tf_op jit(solution)/shard_map/all_to_all | solution.py:48
Sparse Core Ops, SparseCore 0:
  42.9 60.7 reduce-scatter.4
  107.1 34.8 reduce-scatter.6
  167.2 49.8 all-gather.6
  280.4 58.8 reduce-scatter.8
  342.9 34.7 reduce-scatter.10
  403.0 49.8 all-gather.8
where the time goes:
time: 503 us
  waiting for transfers between devices  307 us (61%)
  blocking collectives  133 us (26%)
  starting transfers between devices  22.3 us (4%)
  between operations  15.6 us (3%)
  other arithmetic  11.1 us (2%)
  matrix products  7.85 us (2%)
  local copies, waits for them, and re-layouts  5.99 us (1%)
    reduce_scatter x4, waiting for transfers between devices, own_rows(): running = lax.psum_scatter(running, axis, scatter_dimension=0, tiled=True)  196 us
    all_gather x2, waiting for transfers between devices, gather_in_order(): tiles = lax.all_gather(tiles, axes[k])  99.9 us
    all_gather x2, blocking collectives, body(): column_panel = lax.all_gather(matrix, 'dp', axis=0, tiled=True)  49.4 us
    all_gather x2, blocking collectives, gather_in_order(): tiles = lax.all_gather(tiles, axes[k])  48.5 us
    all_gather x2, blocking collectives, body(): lax.all_gather(mixture, 'dp', axis=0, tiled=True)  35.4 us
    all_to_all x2, starting transfers between devices, from_everyone(): lax.all_to_all(jnp.broadcast_to(x[None], (length, *x.shape)), axis, 0, 0,...  22 us
    all_to_all x2, waiting for transfers between devices, from_everyone(): lax.all_to_all(jnp.broadcast_to(x[None], (length, *x.shape)), axis, 0, 0,...  10.3 us
  transfers between devices with their start and end apart: 8, of which 8 were waited for; matrix products, arithmetic and copies ran while one was open for 1% of the time, Pallas kernels for 0%

commit v1 on v0

v1 whole, which is shorter than its diff:
```python
import math

import jax
import jax.numpy as jnp
from jax import lax
from jax.experimental import pallas as pl
from jax.experimental.pallas import tpu as pltpu
from jax.sharding import Mesh
from jax.sharding import PartitionSpec as P

D = 7168
STEPS = 2
MESH = pl.DeviceIdType.MESH

momentum_decay = 0.95
linear_term = 3.4445
cubic_term = -4.775
quintic_term = 2.0315

SUM_TYPE = jnp.float32


def dot(a, b, dims=(1, 0)):
    return lax.dot_general(a, b, (((dims[0],), (dims[1],)), ((), ())), preferred_element_type=jnp.float32)


def kernel(sizes, start_ref, update_ref, panel, mixed, gram, big_out, big_in, held, small_out, small_in, squares, send_sem, recv_sem):
    nx, nz, ny = sizes
    half_of = (("z", nz), ("y", ny))
    x, core, z, y = (lax.axis_index(a) for a in ("x", "core", "z", "y"))
    place = {"x": x, "z": z, "y": y}
    dp = 2 * x + core
    sign = 1 - 2 * core
    rows = gram.shape[-1]

    def around(p, n):
        return lax.rem(p + 2 * n, n)

    def to(axis, n, step):
        return {axis: around(place[axis] + step, n)}

    barrier = pltpu.get_barrier_semaphore()
    for axis, n in half_of:
        for step in (1, -1):
            pl.semaphore_signal(barrier, inc=1, device_id=to(axis, n, step), device_id_type=MESH)
    for k in range(1, 2 * nx):
        other = lax.rem(dp + k, 2 * nx)
        pl.semaphore_signal(barrier, inc=1, device_id={"x": other // 2, "core": other % 2}, device_id_type=MESH)
    pl.semaphore_wait(barrier, 4 + 2 * nx - 1)

    sent = []

    def send(src, dst, device):
        k = len(sent)
        copy = pltpu.make_async_remote_copy(
            src_ref=src, dst_ref=dst, send_sem=send_sem.at[k], recv_sem=recv_sem.at[k], device_id=device, device_id_type=MESH
        )
        copy.start()
        sent.append(copy)
        return copy

    def ring_gather(axis, n, at, then):
        p = place[axis]
        ways = [[sign, n // 2, None], [-sign, (n - 1) // 2, None]]
        for t in range(n // 2 + 1):
            for way in ways:
                s, count, copy = way
                if t > count:
                    continue
                owner = around(p - s * t, n)
                if t > 0:
                    copy.wait_recv()
                if t < count:
                    way[2] = send(at(owner), at(owner), to(axis, n, s))
                if t > 0:
                    then(owner)
            yield

    def ring_sum(axis, n, local, out, into, add_type):
        p = place[axis]
        ways = [[sign, n // 2, None, 0], [-sign, (n - 1) // 2, None, n // 2]]
        for t in range(n // 2):
            for way in ways:
                s, count, copy, base = way
                if t >= count:
                    continue
                q = around(p + s * (count - t), n)
                value = local(q)
                if t > 0:
                    copy.wait_recv()
                    value = value + into[base + t - 1].astype(jnp.float32)
                out[base + t] = value.astype(add_type)
                way[2] = send(out.at[base + t], into.at[base + t], to(axis, n, s))
            yield
        value = local(p)
        for s, count, copy, base in ways:
            if count:
                copy.wait_recv()
                value = value + into[base + count - 1].astype(jnp.float32)
        yield value

    def together(*parts):
        last = [None] * len(parts)
        live = list(range(len(parts)))
        while live:
            for k in list(live):
                try:
                    last[k] = next(parts[k])
                except StopIteration:
                    live.remove(k)
        return last

    def gather_dp(buf):
        sibling = []

        def pass_on(owner):
            b = 2 * owner + core
            sibling.append(send(buf.at[b], buf.at[b], {"core": 1 - core}))

        ring = ring_gather("x", nx, lambda o: buf.at[2 * o + core], pass_on)
        next(ring)
        pass_on(x)
        together(ring)
        for copy in sibling:
            copy.wait_recv()

    current = start_ref[...]
    for it in range(STEPS):
        matrix = current.astype(jnp.bfloat16)
        wide, mix, g = panel.at[it], mixed.at[it], gram.at[it]
        wide[dp] = matrix
        gather_dp(wide)

        def local_of(first):
            return lambda q: dot(wide[first + q], wide[dp], (0, 0))

        sums = together(
            *(
                ring_sum(axis, n, local_of(h * nz), big_out.at[it, h], big_in.at[it, h], big_out.dtype)
                for h, (axis, n) in enumerate(half_of)
            )
        )
        part = rows // nz
        for h in range(2):
            held[h] = sums[h]

        def part_of(h):
            return lambda q: held[h, pl.ds(pl.multiple_of(q * part, part), part), :]

        crossed = (half_of[1], half_of[0])
        tiles = together(
            *(
                ring_sum(axis, n, part_of(h), small_out.at[it, h], small_in.at[it, h], small_out.dtype)
                for h, (axis, n) in enumerate(crossed)
            )
        )
        own = (z, nz + y)

        def tile_of(h):
            return lambda q: g.at[own[h], pl.ds(pl.multiple_of(q * part, part), part), :]

        for h, (axis, n) in enumerate(crossed):
            tile_of(h)(place[axis])[...] = tiles[h].astype(jnp.bfloat16)
        together(*(ring_gather(axis, n, tile_of(h), lambda o: None) for h, (axis, n) in enumerate(crossed)))

        square, first = [], []

        def use(block):
            value = g[block]
            v = value.astype(jnp.float32)
            v = (v * v).reshape(rows // 8, 8, rows).sum(axis=0)
            square.append(v[:, : rows // 2] + v[:, rows // 2 :])
            first.append(dot(wide[block], value))
            if len(first) > 1:
                square[:] = [square[0] + square[1]]
                first[:] = [first[0] + first[1]]

        rings = [
            ring_gather(axis, n, lambda o, h=h: g.at[h * nz + o], lambda o, h=h: use(h * nz + o))
            for h, (axis, n) in enumerate(half_of)
        ]
        for ring in rings:
            next(ring)
        use(own[0])
        use(own[1])
        together(*rings)

        squares[it, dp] = square[0]
        told = []
        for k in range(1, 2 * nx):
            other = lax.rem(dp + k, 2 * nx)
            told.append(send(squares.at[it, dp], squares.at[it, dp], {"x": other // 2, "core": other % 2}))
        for copy in told:
            copy.wait_recv()
        total = jnp.sum(squares[it], axis=0)
        total = jnp.sum(jnp.sum(total, axis=1, keepdims=True), axis=0, keepdims=True)
        inverse_norm = lax.rsqrt(total)
        root_scale = jnp.sqrt(inverse_norm)
        matrix_full = matrix.astype(jnp.float32)
        mix[dp] = (
            cubic_term * root_scale * matrix_full + quintic_term * root_scale * inverse_norm * first[0]
        ).astype(jnp.bfloat16)
        gather_dp(mix)
        second = dot(mix[0], g[0])
        for j in range(1, 2 * nx):
            second = second + dot(mix[j], g[j])
        current = linear_term * root_scale * matrix_full + inverse_norm * second
    update_ref[...] = math.sqrt(D) * current
    for copy in sent:
        copy.wait_send()


def body(sizes, momentum, gradient):
    nx, nz, ny = sizes
    grad_full = gradient.T.astype(jnp.float32)
    new_momentum = momentum_decay * momentum.T + grad_full
    current = grad_full + momentum_decay * new_momentum
    columns, rows = current.shape
    part = rows // nz
    copies = STEPS * 110
    update = pl.pallas_call(
        lambda *refs: kernel(sizes, *refs),
        out_shape=jax.ShapeDtypeStruct((columns, rows), jnp.float32),
        in_specs=[pl.BlockSpec(memory_space=pltpu.VMEM)],
        out_specs=pl.BlockSpec(memory_space=pltpu.VMEM),
        scratch_shapes=[
            pltpu.VMEM((STEPS, 2 * nx, columns, rows), jnp.bfloat16),
            pltpu.VMEM((STEPS, 2 * nx, columns, rows), jnp.bfloat16),
            pltpu.VMEM((STEPS, nz + ny, rows, rows), jnp.bfloat16),
            pltpu.VMEM((STEPS, 2, nz - 1, rows, rows), SUM_TYPE),
            pltpu.VMEM((STEPS, 2, nz - 1, rows, rows), SUM_TYPE),
            pltpu.VMEM((2, rows, rows), jnp.float32),
            pltpu.VMEM((STEPS, 2, nz - 1, part, rows), jnp.float32),
            pltpu.VMEM((STEPS, 2, nz - 1, part, rows), jnp.float32),
            pltpu.VMEM((STEPS, 2 * nx, 8, rows // 2), jnp.float32),
            pltpu.SemaphoreType.DMA((copies,)),
            pltpu.SemaphoreType.DMA((copies,)),
        ],
        compiler_params=pltpu.CompilerParams(collective_id=0, has_side_effects=True, vmem_limit_bytes=52 * 2**20),
    )(current)
    return new_momentum.T, update.T


def solution(mesh):
    split = Mesh(mesh.devices.reshape(8, 2, 8, 8), ("x", "core", "z", "y"))
    spec = P(("x", "core"), ("z", "y"))
    return jax.shard_map(
        lambda m, g: body((8, 8, 8), m, g),
        mesh=split,
        in_specs=(spec, spec),
        out_specs=(spec, spec),
        check_vma=False,
    )
```

time: 503 us -> 248 us (0.49)
  waiting for transfers between devices: 307 us -> 0 us
  Pallas kernels: 0 us -> 245 us
  blocking collectives: 133 us -> 0 us
  starting transfers between devices: 22.3 us -> 0 us
  between operations: 15.6 us -> 0.67 us
  other arithmetic: 11.1 us -> 1.62 us
  matrix products: 7.85 us -> 0 us
  local copies, waits for them, and re-layouts: 5.99 us -> 0.66 us
    pallas_call x0 -> x1, Pallas kernels: none -> 245 us  [body(): pl.pallas_call(lambda *refs: kernel(sizes, *refs), out_shape=jax.ShapeDty...]
    reduce_scatter x4 -> x0, waiting for transfers between devices: 196 us -> none  [own_rows(): running = lax.psum_scatter(running, axis, scatter_dimension=0, tiled=True)]
    all_gather x6 -> x0, blocking collectives: 133 us -> none  [the longest x2 49.4 us: body(): column_panel = lax.all_gather(matrix, 'dp', axis=0, tiled=True)]
    all_gather x2 -> x0, waiting for transfers between devices: 99.9 us -> none  [gather_in_order(): tiles = lax.all_gather(tiles, axes[k])]
    all_to_all x2 -> x0, starting transfers between devices: 22 us -> none  [from_everyone(): lax.all_to_all(jnp.broadcast_to(x[None], (length, *x.shape)), axis, 0, 0,...]
    all_to_all x2 -> x0, waiting for transfers between devices: 10.3 us -> none  [from_everyone(): lax.all_to_all(jnp.broadcast_to(x[None], (length, *x.shape)), axis, 0, 0,...]
    dot_general x6 -> x0, matrix products: 7.85 us -> none  [the longest x2 5.35 us: body(): lax.dot_general(column_panel, matrix, (((1,), (1,)), ((), ())), preferred...]
    reduce_sum x4 -> x0, other arithmetic: 7.8 us -> none  [the longest x2 6.56 us: body(): jnp.sum(jnp.square(gram_panel.astype(jnp.float32)))]
  transfers between devices with their start and end apart: 8 -> 0, of which waited for: 8 -> 0; matrix products, arithmetic and copies ran while one was open for 1% -> 0% of each run, Pallas kernels for 0% -> 0%
where the time goes in v1:
time: 248 us
  Pallas kernels  245 us (99%)
    pallas_call x1, Pallas kernels, body(): pl.pallas_call(lambda *refs: kernel(sizes, *refs), out_shape=jax.ShapeDty...  245 us

profile of v1, /device:TPU:1, one launch (start us, length us, event | category | flops | bytes accessed | tf_op | source)
XLA Modules:
  0.0 248.1 jit_solution(7564943188469361027)
XLA Ops:
  0.6 1.0 fusion.refs_0_
  1.6 0.0 copy-start
  1.6 0.0 copy-start.1
  1.6 245.1 %shard_map.41 = f32[112,256]{1,0:T(8,128)S(1)} custom-call(f32[112,256]{1,0:T(8,128)S(1)} %fusion.refs_0_), custom_call_target="tpu_custom_call" | custom-call | tf_op jit(solution)/shard_map/pallas_call | solution.py:221
  246.7 0.0 copy-done
  246.8 0.0 copy-done.1
  246.8 0.7 convert_add_fusion
  247.4 0.6 copy.5
Async XLA Ops:
  1.6 245.2 %copy-start = (f32[256,112]{0,1:T(8,128)S(1)}, f32[256,112]{0,1:T(8,128)}, u32[]{:S(2)}) copy-start(f32[256,112]{0,1:T(8,128)} %param.2) | copy-start | bytes 344068
  1.6 245.2 %copy-start.1 = (bf16[256,112]{0,1:T(8,128)(2,1)S(1)}, bf16[256,112]{0,1:T(8,128)(2,1)}, u32[]{:S(2)}) copy-start(bf16[256,112]{0,1:T(8,128)(2,1)} %param.3) | copy-start | bytes 172036

commit v2 on v1

--- a/solution.py
+++ b/solution.py
@@ -17,7 +17,9 @@
 cubic_term = -4.775
 quintic_term = 2.0315
 
-SUM_TYPE = jnp.float32
+SUM_TYPE = jnp.bfloat16
+SMALL = jnp.bfloat16
+SUBS = 2
 
 
 def dot(a, b, dims=(1, 0)):
@@ -41,12 +43,12 @@
 
     barrier = pltpu.get_barrier_semaphore()
     for axis, n in half_of:
-        for step in (1, -1):
+        for step in range(1, n):
             pl.semaphore_signal(barrier, inc=1, device_id=to(axis, n, step), device_id_type=MESH)
     for k in range(1, 2 * nx):
         other = lax.rem(dp + k, 2 * nx)
         pl.semaphore_signal(barrier, inc=1, device_id={"x": other // 2, "core": other % 2}, device_id_type=MESH)
-    pl.semaphore_wait(barrier, 4 + 2 * nx - 1)
+    pl.semaphore_wait(barrier, nz + ny + 2 * nx - 3)
 
     sent = []
 
@@ -99,6 +101,18 @@
                 value = value + into[base + count - 1].astype(jnp.float32)
         yield value
 
+    def far_first(n):
+        return sorted(range(1, n), key=lambda k: -min(k, n - k))
+
+    def direct_gather(axis, n, at):
+        own = at(place[axis])
+        return [send(own, own, to(axis, n, k)) for k in far_first(n)]
+
+    def direct_sum(axis, n, local, into):
+        p = place[axis]
+        copies = [send(local(around(p + k, n)), into.at[k - 1], to(axis, n, k)) for k in far_first(n)]
+        return copies, into
+
     def together(*parts):
         last = [None] * len(parts)
         live = list(range(len(parts)))
@@ -113,14 +127,36 @@
     def gather_dp(buf):
         sibling = []
 
+        def at(owner):
+            return buf.at[2 * owner + core]
+
         def pass_on(owner):
-            b = 2 * owner + core
-            sibling.append(send(buf.at[b], buf.at[b], {"core": 1 - core}))
-
-        ring = ring_gather("x", nx, lambda o: buf.at[2 * o + core], pass_on)
-        next(ring)
+            sibling.append(send(at(owner), at(owner), {"core": 1 - core}))
+
+        def go(owner, step):
+            return send(at(owner), at(owner), to("x", nx, step))
+
+        ways = (sign, -sign)
+        twos = [go(x, 2 * s) for s in ways]
+        ones = [go(x, s) for s in ways]
         pass_on(x)
-        together(ring)
+        threes = []
+        for s, copy in zip(ways, twos):
+            copy.wait_recv()
+            owner = around(x - 2 * s, nx)
+            if len(threes) == 0:
+                four = go(owner, 2 * s)
+            threes.append(go(owner, s))
+        for s, copy in zip(ways, ones):
+            copy.wait_recv()
+            pass_on(around(x - s, nx))
+        for s in ways:
+            pass_on(around(x - 2 * s, nx))
+        for s, copy in zip(ways, threes):
+            copy.wait_recv()
+            pass_on(around(x - 3 * s, nx))
+        four.wait_recv()
+        pass_on(around(x + 4, nx))
         for copy in sibling:
             copy.wait_recv()
 
@@ -131,68 +167,95 @@
         wide[dp] = matrix
         gather_dp(wide)
 
-        def local_of(first):
-            return lambda q: dot(wide[first + q], wide[dp], (0, 0))
-
+        sub = rows // SUBS
+        turned = matrix.T
+
+        def local_of(first, b):
+            return lambda q: dot(turned[b * sub : (b + 1) * sub], wide[first + q])
+
+        parts = [(h, b) for b in range(SUBS) for h in range(2)]
         sums = together(
             *(
-                ring_sum(axis, n, local_of(h * nz), big_out.at[it, h], big_in.at[it, h], big_out.dtype)
-                for h, (axis, n) in enumerate(half_of)
+                ring_sum(*half_of[h], local_of(h * nz, b), big_out.at[it, h, b], big_in.at[it, h, b], big_out.dtype)
+                for h, b in parts
             )
         )
         part = rows // nz
-        for h in range(2):
-            held[h] = sums[h]
-
-        def part_of(h):
-            return lambda q: held[h, pl.ds(pl.multiple_of(q * part, part), part), :]
+        whole = held.at[it]
+        for (h, b), value in zip(parts, sums):
+            whole[h, b * sub : (b + 1) * sub] = value
+            small_out[it, h, b * sub : (b + 1) * sub] = value.astype(SMALL)
+        def part_of(h, of):
+            return lambda q: of.at[h, pl.ds(pl.multiple_of(q * part, part), part), :]
 
         crossed = (half_of[1], half_of[0])
-        tiles = together(
-            *(
-                ring_sum(axis, n, part_of(h), small_out.at[it, h], small_in.at[it, h], small_out.dtype)
-                for h, (axis, n) in enumerate(crossed)
-            )
-        )
+        started = [direct_sum(*crossed[h], part_of(h, small_out.at[it]), small_in.at[it, h]) for h in range(2)]
         own = (z, nz + y)
 
         def tile_of(h):
             return lambda q: g.at[own[h], pl.ds(pl.multiple_of(q * part, part), part), :]
 
-        for h, (axis, n) in enumerate(crossed):
-            tile_of(h)(place[axis])[...] = tiles[h].astype(jnp.bfloat16)
-        together(*(ring_gather(axis, n, tile_of(h), lambda o: None) for h, (axis, n) in enumerate(crossed)))
-
-        square, first = [], []
+        square = jnp.zeros((8, rows // 2), jnp.float32)
+        arriving = []
+        for h in range(2):
+            axis, n = crossed[h]
+            copies, into = started[h]
+            value = part_of(h, whole)(place[axis])[...]
+            for copy in copies:
+                copy.wait_recv()
+            tile = (value + jnp.sum(into[...].astype(jnp.float32), axis=0)).astype(jnp.bfloat16)
+            tile_of(h)(place[axis])[...] = tile
+            arriving += direct_gather(axis, n, tile_of(h))
+            v = tile.astype(jnp.float32)
+            v = (v * v).reshape(part // 8, 8, rows).sum(axis=0)
+            square = square + v[:, : rows // 2] + v[:, rows // 2 :]
+        told = []
+        squares[it, 0, 0] = square
+        for k in range(1, 2 * nx):
+            other = lax.rem(dp + k, 2 * nx)
+            told.append(send(squares.at[it, 0, 0], squares.at[it, 0, k], {"x": other // 2, "core": other % 2}))
+
+        def spread(stage, axis, n):
+            for copy in told:
+                copy.wait_recv()
+            count = 2 * nx if stage == 1 else n
+            squares[it, stage, 0] = jnp.sum(squares[it, stage - 1, :count], axis=0)
+            told[:] = [
+                send(squares.at[it, stage, 0], squares.at[it, stage, k], to(axis, n, k)) for k in range(1, n)
+            ]
+
+        for copy in arriving:
+            copy.wait_recv()
+
+        first = []
 
         def use(block):
-            value = g[block]
-            v = value.astype(jnp.float32)
-            v = (v * v).reshape(rows // 8, 8, rows).sum(axis=0)
-            square.append(v[:, : rows // 2] + v[:, rows // 2 :])
-            first.append(dot(wide[block], value))
+            first.append(dot(wide[block], g[block], (1, 1)))
             if len(first) > 1:
-                square[:] = [square[0] + square[1]]
                 first[:] = [first[0] + first[1]]
 
         rings = [
-            ring_gather(axis, n, lambda o, h=h: g.at[h * nz + o], lambda o, h=h: use(h * nz + o))
-            for h, (axis, n) in enumerate(half_of)
+            ring_gather(
+                *half_of[h],
+                lambda o, h=h, b=b: g.at[h * nz + o, b * sub : (b + 1) * sub],
+                lambda o, h=h, b=b: use(h * nz + o) if b == SUBS - 1 else None,
+            )
+            for h, b in parts
         ]
         for ring in rings:
             next(ring)
         use(own[0])
         use(own[1])
+        spread(1, "z", nz)
+        for ring in rings:
+            next(ring)
+        for ring in rings:
+            next(ring)
+        spread(2, "y", ny)
         together(*rings)
-
-        squares[it, dp] = square[0]
-        told = []
-        for k in range(1, 2 * nx):
-            other = lax.rem(dp + k, 2 * nx)
-            told.append(send(squares.at[it, dp], squares.at[it, dp], {"x": other // 2, "core": other % 2}))
         for copy in told:
             copy.wait_recv()
-        total = jnp.sum(squares[it], axis=0)
+        total = jnp.sum(squares[it, 2, :ny], axis=0)
         total = jnp.sum(jnp.sum(total, axis=1, keepdims=True), axis=0, keepdims=True)
         inverse_norm = lax.rsqrt(total)
         root_scale = jnp.sqrt(inverse_norm)
@@ -201,9 +264,9 @@
             cubic_term * root_scale * matrix_full + quintic_term * root_scale * inverse_norm * first[0]
         ).astype(jnp.bfloat16)
         gather_dp(mix)
-        second = dot(mix[0], g[0])
+        second = dot(mix[0], g[0], (1, 1))
         for j in range(1, 2 * nx):
-            second = second + dot(mix[j], g[j])
+            second = second + dot(mix[j], g[j], (1, 1))
         current = linear_term * root_scale * matrix_full + inverse_norm * second
     update_ref[...] = math.sqrt(D) * current
     for copy in sent:
@@ -217,7 +280,7 @@
     current = grad_full + momentum_decay * new_momentum
     columns, rows = current.shape
     part = rows // nz
-    copies = STEPS * 110
+    copies = STEPS * 150
     update = pl.pallas_call(
         lambda *refs: kernel(sizes, *refs),
         out_shape=jax.ShapeDtypeStruct((columns, rows), jnp.float32),
@@ -227,12 +290,12 @@
             pltpu.VMEM((STEPS, 2 * nx, columns, rows), jnp.bfloat16),
             pltpu.VMEM((STEPS, 2 * nx, columns, rows), jnp.bfloat16),
             pltpu.VMEM((STEPS, nz + ny, rows, rows), jnp.bfloat16),
-            pltpu.VMEM((STEPS, 2, nz - 1, rows, rows), SUM_TYPE),
-            pltpu.VMEM((STEPS, 2, nz - 1, rows, rows), SUM_TYPE),
-            pltpu.VMEM((2, rows, rows), jnp.float32),
-            pltpu.VMEM((STEPS, 2, nz - 1, part, rows), jnp.float32),
-            pltpu.VMEM((STEPS, 2, nz - 1, part, rows), jnp.float32),
-            pltpu.VMEM((STEPS, 2 * nx, 8, rows // 2), jnp.float32),
+            pltpu.VMEM((STEPS, 2, SUBS, nz - 1, rows // SUBS, rows), SUM_TYPE),
+            pltpu.VMEM((STEPS, 2, SUBS, nz - 1, rows // SUBS, rows), SUM_TYPE),
+            pltpu.VMEM((STEPS, 2, rows, rows), jnp.float32),
+            pltpu.VMEM((STEPS, 2, rows, rows), SMALL),
+            pltpu.VMEM((STEPS, 2, nz - 1, part, rows), SMALL),
+            pltpu.VMEM((STEPS, 3, 2 * nx, 8, rows // 2), jnp.float32),
             pltpu.SemaphoreType.DMA((copies,)),
             pltpu.SemaphoreType.DMA((copies,)),
         ],

time: 248 us -> 169 us (0.68)
  Pallas kernels: 245 us -> 166 us
    pallas_call x1, Pallas kernels: 245 us -> 166 us  [body(): pl.pallas_call(lambda *refs: kernel(sizes, *refs), out_shape=jax.ShapeDty...]
where the time goes in v2:
time: 169 us
  Pallas kernels  166 us (98%)
    pallas_call x1, Pallas kernels, body(): pl.pallas_call(lambda *refs: kernel(sizes, *refs), out_shape=jax.ShapeDty...  166 us

profile of v2, /device:TPU:1, one launch (start us, length us, event | category | flops | bytes accessed | tf_op | source)
XLA Modules:
  0.0 168.6 jit_solution(16560602712411608155)
XLA Ops:
  0.6 1.0 fusion.refs_0_
  1.6 0.0 copy-start
  1.6 0.0 copy-start.1
  1.6 165.7 %shard_map.41 = f32[112,256]{1,0:T(8,128)S(1)} custom-call(f32[112,256]{1,0:T(8,128)S(1)} %fusion.refs_0_), custom_call_target="tpu_custom_call" | custom-call | tf_op jit(solution)/shard_map/pallas_call | solution.py:284
  167.3 0.0 copy-done
  167.3 0.0 copy-done.1
  167.3 0.7 convert_add_fusion
  168.0 0.6 copy.5
Async XLA Ops:
  1.6 165.7 %copy-start = (f32[256,112]{0,1:T(8,128)S(1)}, f32[256,112]{0,1:T(8,128)}, u32[]{:S(2)}) copy-start(f32[256,112]{0,1:T(8,128)} %param.2) | copy-start | bytes 344068
  1.6 165.7 %copy-start.1 = (bf16[256,112]{0,1:T(8,128)(2,1)S(1)}, bf16[256,112]{0,1:T(8,128)(2,1)}, u32[]{:S(2)}) copy-start(bf16[256,112]{0,1:T(8,128)(2,1)} %param.3) | copy-start | bytes 172036

commit v3 on v2

--- a/solution.py
+++ b/solution.py
@@ -20,6 +20,7 @@
 SUM_TYPE = jnp.bfloat16
 SMALL = jnp.bfloat16
 SUBS = 2
+SUM_SUBS = 4
 
 
 def dot(a, b, dims=(1, 0)):
@@ -170,21 +171,24 @@
         sub = rows // SUBS
         turned = matrix.T
 
+        thin = rows // SUM_SUBS
+
         def local_of(first, b):
-            return lambda q: dot(turned[b * sub : (b + 1) * sub], wide[first + q])
+            return lambda q: dot(turned[b * thin : (b + 1) * thin], wide[first + q])
 
         parts = [(h, b) for b in range(SUBS) for h in range(2)]
+        sum_parts = [(h, b) for b in range(SUM_SUBS) for h in range(2)]
         sums = together(
             *(
                 ring_sum(*half_of[h], local_of(h * nz, b), big_out.at[it, h, b], big_in.at[it, h, b], big_out.dtype)
-                for h, b in parts
+                for h, b in sum_parts
             )
         )
         part = rows // nz
         whole = held.at[it]
-        for (h, b), value in zip(parts, sums):
-            whole[h, b * sub : (b + 1) * sub] = value
-            small_out[it, h, b * sub : (b + 1) * sub] = value.astype(SMALL)
+        for (h, b), value in zip(sum_parts, sums):
+            whole[h, b * thin : (b + 1) * thin] = value
+            small_out[it, h, b * thin : (b + 1) * thin] = value.astype(SMALL)
         def part_of(h, of):
             return lambda q: of.at[h, pl.ds(pl.multiple_of(q * part, part), part), :]
 
@@ -280,7 +284,7 @@
     current = grad_full + momentum_decay * new_momentum
     columns, rows = current.shape
     part = rows // nz
-    copies = STEPS * 150
+    copies = STEPS * 175
     update = pl.pallas_call(
         lambda *refs: kernel(sizes, *refs),
         out_shape=jax.ShapeDtypeStruct((columns, rows), jnp.float32),
@@ -290,8 +294,8 @@
             pltpu.VMEM((STEPS, 2 * nx, columns, rows), jnp.bfloat16),
             pltpu.VMEM((STEPS, 2 * nx, columns, rows), jnp.bfloat16),
             pltpu.VMEM((STEPS, nz + ny, rows, rows), jnp.bfloat16),
-            pltpu.VMEM((STEPS, 2, SUBS, nz - 1, rows // SUBS, rows), SUM_TYPE),
-            pltpu.VMEM((STEPS, 2, SUBS, nz - 1, rows // SUBS, rows), SUM_TYPE),
+            pltpu.VMEM((STEPS, 2, SUM_SUBS, nz - 1, rows // SUM_SUBS, rows), SUM_TYPE),
+            pltpu.VMEM((STEPS, 2, SUM_SUBS, nz - 1, rows // SUM_SUBS, rows), SUM_TYPE),
             pltpu.VMEM((STEPS, 2, rows, rows), jnp.float32),
             pltpu.VMEM((STEPS, 2, rows, rows), SMALL),
             pltpu.VMEM((STEPS, 2, nz - 1, part, rows), SMALL),

time: 169 us -> 168 us (level)
  no operation moved by 1% of the time
where the time goes in v3:
time: 168 us
  Pallas kernels  165 us (98%)
    pallas_call x1, Pallas kernels, body(): pl.pallas_call(lambda *refs: kernel(sizes, *refs), out_shape=jax.ShapeDty...  165 us

profile of v3, /device:TPU:1, one launch (start us, length us, event | category | flops | bytes accessed | tf_op | source)
XLA Modules:
  0.0 167.7 jit_solution(16474217872413953038)
XLA Ops:
  0.6 1.0 fusion.refs_0_
  1.6 0.0 copy-start
  1.6 0.0 copy-start.1
  1.6 164.7 %shard_map.41 = f32[112,256]{1,0:T(8,128)S(1)} custom-call(f32[112,256]{1,0:T(8,128)S(1)} %fusion.refs_0_), custom_call_target="tpu_custom_call" | custom-call | tf_op jit(solution)/shard_map/pallas_call | solution.py:288
  166.3 0.0 copy-done
  166.3 0.0 copy-done.1
  166.3 0.7 convert_add_fusion
  167.0 0.6 copy.5
Async XLA Ops:
  1.6 164.7 %copy-start = (f32[256,112]{0,1:T(8,128)S(1)}, f32[256,112]{0,1:T(8,128)}, u32[]{:S(2)}) copy-start(f32[256,112]{0,1:T(8,128)} %param.2) | copy-start | bytes 344068
  1.6 164.7 %copy-start.1 = (bf16[256,112]{0,1:T(8,128)(2,1)S(1)}, bf16[256,112]{0,1:T(8,128)(2,1)}, u32[]{:S(2)}) copy-start(bf16[256,112]{0,1:T(8,128)(2,1)} %param.3) | copy-start | bytes 172036
